TPU v7x, 256 devices: a whole 4x4x8 slice. The times are simulated.
256 devices in a mesh: br: 64 (over z, y, core), hd: 4 (over x).
Axes of the slice: x: 4, y: 4, z: 8, core: 2. Of those that a mesh axis runs over, the one named last changes fastest.
Arguments:
- branch_q: bfloat16 [32768, 5120], P('br', 'hd'), may hold values from -600 to 600
- branch_k: bfloat16 [32768, 5120], P('br', 'hd'), may hold values from -6 to 6
- branch_v: bfloat16 [32768, 5120], P('br', 'hd'), may hold values from -6 to 6
- branch_out: bfloat16 [32768, 5120], P('br', 'hd'), may hold values from -6 to 6
- branch_grad: bfloat16 [32768, 5120], P('br', 'hd'), may hold values from -6 to 6
- prefix_k: bfloat16 [2, 256, 5120], P(None, 'hd'), may hold values from -6 to 6
- prefix_v: bfloat16 [2, 256, 5120], P(None, 'hd'), may hold values from -6 to 6
- parents: int32 [64, 4], P('br'), may hold values from -1 to 2, as said below
- lengths: int32 [64, 4], P('br'), may hold values from 1 to 128, as said below
- prompt_of: int32 [64, 1], replicated, may hold values from 0 to 1
Outputs:
- branch_dq: bfloat16 [32768, 5120], P('br', 'hd')
- branch_dk: bfloat16 [32768, 5120], P('br', 'hd')
- branch_dv: bfloat16 [32768, 5120], P('br', 'hd')
- prefix_dk: bfloat16 [2, 256, 5120], P(None, 'hd')
- prefix_dv: bfloat16 [2, 256, 5120], P(None, 'hd')
Inputs may be any that keep to these rules, and one draw needn't show every extreme that they name: `parents`: every parent is below its own block; each tree's last block has the block before it as parent. `lengths`: each tree's first block is full; the first tree's last block holds one token.
All inputs are finite; a program needn't handle non-finite values.
Results may differ from a plain program's by a relative error of at most 0.0075.
Values may be sent and summed in bfloat16 or wider, within the bound.
A program may use at most 128 MiB of HBM per device.

v0:
```python
import jax
import jax.numpy as jnp
from jax import lax
from jax.sharding import PartitionSpec as P

HS = 128
TILE = 128


neg_fill = -1e30


def ancestors(parents, blocks):
    block_ids = jnp.arange(blocks, dtype=jnp.int32)
    parent_hit = parents[:, None] == block_ids[None, :]

    def extend(sweep_num, found_set):
        return found_set | jnp.any(found_set[:, :, None] & parent_hit[None, :, :], axis=1)

    return lax.fori_loop(0, blocks, extend, parent_hit)


def tree_masks(parents, lengths, tile_rows, prefix_len):
    blocks = parents.shape[0]
    ancestor = ancestors(parents, blocks)
    row_count = blocks * tile_rows
    row_index = jnp.arange(row_count, dtype=jnp.int32)
    block_of = row_index // tile_rows
    offset = row_index % tile_rows
    fill_count = jnp.repeat(lengths, tile_rows)
    live_rows = offset < fill_count
    same_block = block_of[:, None] == block_of[None, :]
    earlier = offset[None, :] <= offset[:, None]
    wide_above = jnp.repeat(jnp.repeat(ancestor, tile_rows, axis=0), tile_rows, axis=1)
    allowed = live_rows[None, :] & (wide_above | same_block & earlier)
    full_mask = jnp.concatenate([jnp.ones((row_count, prefix_len), dtype=bool), allowed], axis=1)
    return (full_mask, live_rows)


def head_grads(queries, key_rows, value_rows, output, cotangent, full_mask, live_rows, scaling):
    scores = jnp.dot(queries, key_rows.T, preferred_element_type=jnp.float32) * scaling
    scores = jnp.where(full_mask, scores, neg_fill)
    row_max = jnp.max(scores, axis=1, keepdims=True)
    shifted = jnp.exp(scores - row_max)
    attention = shifted / jnp.sum(shifted, axis=1, keepdims=True)
    attention_low = attention.astype(jnp.bfloat16)
    kept_grad = jnp.where(live_rows[:, None], cotangent, jnp.zeros_like(cotangent))
    dvalues = jnp.dot(attention_low.T, kept_grad, preferred_element_type=jnp.float32)
    dattention = jnp.dot(kept_grad, value_rows.T, preferred_element_type=jnp.float32)
    row_dot = jnp.sum(
        kept_grad.astype(jnp.float32) * output.astype(jnp.float32), axis=1, keepdims=True
    )
    dscore = (attention * (dattention - row_dot)).astype(jnp.bfloat16)
    dquery = jnp.dot(dscore, key_rows, preferred_element_type=jnp.float32) * scaling
    dkey_rows = jnp.dot(dscore.T, queries, preferred_element_type=jnp.float32) * scaling
    return (dquery, dkey_rows, dvalues)


def tree_grads(
    queries,
    branch_keys,
    branch_values,
    output,
    cotangent,
    prompt_keys,
    prompt_values,
    parents,
    lengths,
    head_size,
    tile_rows,
):
    prefix_len = prompt_keys.shape[0]
    full_mask, live_rows = tree_masks(parents, lengths, tile_rows, prefix_len)
    all_keys = jnp.concatenate([prompt_keys, branch_keys], axis=0)
    all_values = jnp.concatenate([prompt_values, branch_values], axis=0)
    head_count = queries.shape[1] // head_size
    scaling = head_size ** (-0.5)
    row_count = queries.shape[0]
    key_total = all_keys.shape[0]
    columns = queries.shape[1]
    zeros_init = (
        jnp.zeros((row_count, columns), jnp.float32),
        jnp.zeros((key_total, columns), jnp.float32),
        jnp.zeros((key_total, columns), jnp.float32),
    )

    def one_head(head_num, partial_value):
        col_start = head_num * head_size

        def slice_cols(array):
            return lax.dynamic_slice_in_dim(array, col_start, head_size, 1)

        dquery, dkey_rows, dvalues = head_grads(
            slice_cols(queries),
            slice_cols(all_keys),
            slice_cols(all_values),
            slice_cols(output),
            slice_cols(cotangent),
            full_mask,
            live_rows,
            scaling,
        )
        return (
            lax.dynamic_update_slice_in_dim(partial_value[0], dquery, col_start, 1),
            lax.dynamic_update_slice_in_dim(partial_value[1], dkey_rows, col_start, 1),
            lax.dynamic_update_slice_in_dim(partial_value[2], dvalues, col_start, 1),
        )

    dquery, dkey_rows, dvalues = lax.fori_loop(0, head_count, one_head, zeros_init)
    return (
        dquery.astype(jnp.bfloat16),
        dkey_rows[prefix_len:].astype(jnp.bfloat16),
        dvalues[prefix_len:].astype(jnp.bfloat16),
        dkey_rows[:prefix_len],
        dvalues[:prefix_len],
    )


def per_device(
    branch_q,
    branch_k,
    branch_v,
    branch_out,
    branch_grad,
    prefix_k,
    prefix_v,
    parents,
    lengths,
    prompt_of,
):
    owners = prompt_of[:, 0]
    groups = lax.axis_size("hd")
    prompts = prefix_k.shape[0]
    own_rows = prefix_k.shape[1]
    full_width = prefix_k.shape[2]
    head_cols = full_width // groups
    prompt_rows = own_rows * groups
    my_index = lax.axis_index("br")
    my_prompt = owners[my_index]

    def own_slab(table):
        chosen = lax.dynamic_index_in_dim(table, my_prompt, 0, keepdims=False)
        return chosen.reshape(own_rows, groups, head_cols)

    moved_keys, moved_values = (
        lax.all_to_all(own_slab(prefix_k), "hd", split_axis=1, concat_axis=0, tiled=True),
        lax.all_to_all(own_slab(prefix_v), "hd", split_axis=1, concat_axis=0, tiled=True),
    )
    prompt_keys = moved_keys.reshape(prompt_rows, head_cols)
    prompt_values = moved_values.reshape(prompt_rows, head_cols)
    dquery, dkey, dvalue, prompt_dk, prompt_dv = tree_grads(
        branch_q,
        branch_k,
        branch_v,
        branch_out,
        branch_grad,
        prompt_keys,
        prompt_values,
        parents[0],
        lengths[0],
        HS,
        TILE,
    )
    selected = (jnp.arange(prompts, dtype=jnp.int32) == my_prompt).astype(jnp.float32)
    slab = jnp.stack([prompt_dk, prompt_dv], axis=1)
    summed = lax.psum(slab[:, :, None, :] * selected[None, None, :, None], "br")
    rounded = summed.astype(jnp.bfloat16)
    arranged = rounded.reshape(groups, own_rows, 2, prompts, 1, head_cols)
    spread = lax.all_to_all(arranged, "hd", split_axis=0, concat_axis=4, tiled=True)
    merged = spread.reshape(own_rows, 2, prompts, full_width)
    prefix_dk = jnp.swapaxes(merged[:, 0], 0, 1)
    prefix_dv = jnp.swapaxes(merged[:, 1], 0, 1)
    return (dquery, dkey, dvalue, prefix_dk, prefix_dv)


def solution(mesh):
    placed = (
        P("br", "hd"),
        P("br", "hd"),
        P("br", "hd"),
        P("br", "hd"),
        P("br", "hd"),
        P(None, "hd", None),
        P(None, "hd", None),
        P("br", None),
        P("br", None),
        P(),
    )
    return jax.shard_map(
        per_device,
        mesh=mesh,
        in_specs=placed,
        out_specs=(
            P("br", "hd"),
            P("br", "hd"),
            P("br", "hd"),
            P(None, "hd", None),
            P(None, "hd", None),
        ),
        check_vma=False,
    )
```

profile of v0, /device:TPU:1, one launch (start us, length us, event | category | flops | bytes accessed | tf_op | source)
XLA Modules:
  0.0 485.8 jit_solution(4458987753376372862)
XLA Ops:
  6.6 4.8 all-to-all-start
  13.7 6.5 %all-to-all-done = bf16[64,4,1280]{2,0,1:T(8,128)(2,1)S(1)} async-done(((bf16[64,4,1280]{2,0,1:T(8,128)(2,1)}), bf16[64,4,1280]{2,0,1:T(8,128)(2,1)S(1)}, u32[]{:S(2)}, u32[]{:S(2)}) %all-to-all-start) | async-done | bytes 655392 | tf_op jit(solution)/shard_map/all_to_all | solution.py:146
  20.2 4.2 all-to-all-start.1
  28.7 3.4 all-to-all-done.1
  32.1 2.9 pad_maximum_fusion.2
  40.5 102.7 %while.30 = (s32[]{:T(128)}, bf16[512,1280]{1,0:T(8,128)(2,1)}, f32[768,1280]{1,0:T(8,128)}, f32[768,1280]{1,0:T(8,128)}, bf16[512,1280]{1,0:T(8,128)(2,1)}, /*i...) while((s32[]{:T(128)}, bf16[512,1280]{1,0:T(8,128)(2,1)}, ...), condition=%wide.region_7.8_spmd.clone, body=%wide.region_3.7_spmd.clone.sunk | while | flops 509052928 | bytes 11494607 | solution.py:109
  46.2 2.4 convolution_dynamic-update-slice_fusion.2
  56.5 2.4 convolution_dynamic-update-slice_fusion.2
  66.8 2.4 convolution_dynamic-update-slice_fusion.2
  77.0 2.4 convolution_dynamic-update-slice_fusion.2
  87.3 2.4 convolution_dynamic-update-slice_fusion.2
  97.5 2.5 convolution_dynamic-update-slice_fusion.2
  107.8 2.5 convolution_dynamic-update-slice_fusion.2
  118.2 2.4 convolution_dynamic-update-slice_fusion.2
  128.4 2.4 convolution_dynamic-update-slice_fusion.2
  138.7 2.4 convolution_dynamic-update-slice_fusion.2
  146.2 2.8 broadcast_multiply_fusion
  149.0 295.7 %all-reduce.2 = bf16[256,2,2,1280]{3,0,2,1:T(8,128)(2,1)S(1)} all-reduce(f32[256,2,2,1280]{3,0,2,1:T(8,128)} %broadcast_multiply_fusion), channel_id=1, replica_groups=mesh['br'=64,'hd'=4] {'br'}, use_global_device_ids=true, to_apply=%region_8.9 | all-reduce | flops 1310720 | bytes 7864320 | tf_op jit(solution)/shard_map/psum | solution.py:166
  446.4 3.7 all-to-all-start.2
  450.0 2.9 slice.36
  453.0 2.9 slice.37
  455.9 20.1 %all-to-all-done.2 = bf16[4,64,2,2,1,1280]{5,1,3,2,4,0:T(8,128)(2,1)S(1)} async-done(((bf16[4,64,2,2,1,1280]{5,1,3,2,4,0:T(8,128)(2,1)}), bf16[4,64,2,2,1,1280]{5,1,3,2,4,0:T(8,128)(2,1)S(1)}, u32[]{:S(2)}, u32[]{:S(2)}) %all-to-all-start.2) | async-done | bytes 2621472 | tf_op jit(solution)/shard_map/all_to_all | solution.py:169
  476.0 3.5 copy.26
  479.6 4.5 reshape.116
  (113 shorter events, 101.5 us)
Async XLA Ops:
  0.6 0.7 copy-start
  5.7 5.8 %copy-start.1 = (s32[1,4]{1,0:T(1,128)S(1)}, s32[1,4]{1,0:T(1,128)}, u32[]{:S(2)}) copy-start(s32[1,4]{1,0:T(1,128)} %param.21) | copy-start | bytes 52
  6.6 13.6 %all-to-all-start = ((bf16[64,4,1280]{2,0,1:T(8,128)(2,1)}), bf16[64,4,1280]{2,0,1:T(8,128)(2,1)S(1)}, u32[]{:S(2)}, u32[]{:S(2)}) async-start(bf16[64,4,1280]{2,0,1:T(8,128)(2,1)} %copy.23), calls=%async_computation | async-start | bytes 1310720 | tf_op jit(solution)/shard_map/all_to_all | solution.py:146
  11.4 2.2 copy-start.2
  20.2 11.9 %all-to-all-start.1 = ((bf16[64,4,1280]{2,0,1:T(8,128)(2,1)}), bf16[64,4,1280]{2,0,1:T(8,128)(2,1)}, u32[]{:S(2)}, u32[]{:S(2)}) async-start(bf16[64,4,1280]{2,0,1:T(8,128)(2,1)} %copy.24), calls=%async_computation.1 | async-start | bytes 1310720 | tf_op jit(solution)/shard_map/all_to_all | solution.py:147
  446.4 29.7 %all-to-all-start.2 = ((bf16[4,64,2,2,1,1280]{5,1,3,2,4,0:T(8,128)(2,1)}), bf16[4,64,2,2,1,1280]{5,1,3,2,4,0:T(8,128)(2,1)S(1)}, u32[]{:S(2)}, u32[]{:S(2)}) async-start(bf16[4,64,2,2,1,1280]{5,1,3,2,4,0:T(8,128)(2,1)} %copy.25), calls=%async_computation.2 | async-start | bytes 5242880 | tf_op jit(solution)/shard_map/all_to_all | solution.py:169
where the time goes:
time: 492 us; the launch traced here: 486 us
  blocking collectives  296 us (60%)
  matrix products  85.6 us (17%)
  local copies, waits for them, and re-layouts  32.8 us (7%)
  waiting for transfers between devices  30 us (6%)
  other arithmetic  26.2 us (5%)
  starting transfers between devices  12.7 us (3%)
    psum x1, blocking collectives, per_device(): summed = lax.psum(slab[:, :, None, :] * selected[None, None, :, None], 'br')  296 us
    dot_general x10, matrix products, head_grads(): jnp.dot(attention_low.T, kept_grad, preferred_element_type=jnp.float32)  24.2 us
    dot_general x10, matrix products, head_grads(): jnp.dot(dscore.T, queries, preferred_element_type=jnp.float32) * scaling  21.1 us
    all_to_all x1, waiting for transfers between devices, per_device(): lax.all_to_all(arranged, 'hd', split_axis=0, concat_axis=4, tiled=True)  20.1 us
    dot_general x10, matrix products, head_grads(): jnp.dot(kept_grad, value_rows.T, preferred_element_type=jnp.float32)  15.7 us
    dot_general x10, matrix products, head_grads(): jnp.dot(queries, key_rows.T, preferred_element_type=jnp.float32) * scaling  14.2 us
    reduce_sum x10, other arithmetic, head_grads(): jnp.sum(kept_grad.astype(jnp.float32) * output.astype(jnp.float32), axis=...  12 us
    dot_general x10, matrix products, head_grads(): jnp.dot(dscore, key_rows, preferred_element_type=jnp.float32) * scaling  10.4 us
  transfers between devices with their start and end apart: 3, of which 3 were waited for; matrix products, arithmetic and copies ran while one was open for 3% of the time, Pallas kernels for 0%

commit v1 on v0

v1 whole, which is shorter than its diff:
```python
import functools

import jax
import jax.numpy as jnp
from jax import lax
from jax.experimental import pallas as pl
from jax.experimental.pallas import tpu as pltpu
from jax.sharding import PartitionSpec as P

HS = 128
TILE = 128
BLOCKS = 4
PLEN = 256
PROMPTS = 2
ROWS = 512
HEADS = 10
COLS = 1280
GROUPS = 4
NY = 4
NZ = 8
LOG2E = 1.4426950408889634
MESH = pl.DeviceIdType.MESH
VMEM = pltpu.VMEM
WIDTHS = (384, 256)
STARTS = (0, 768)


def place():
    br = lax.axis_index("br")
    core = br % 2
    y = (br // 2) % NY
    z = br // (2 * NY)
    return lax.axis_index("hd"), y, z, core


def device(x, y, z, core):
    return ((z * NY + y) * 2 + core, x)


def greet(partners):
    barrier = pltpu.get_barrier_semaphore()
    for who in partners:
        pl.semaphore_signal(barrier, inc=1, device_id=who, device_id_type=MESH)
    pl.semaphore_wait(barrier, len(partners))


def remote(src, dst, send, recv, who):
    return pltpu.make_async_remote_copy(
        src_ref=src, dst_ref=dst, send_sem=send, recv_sem=recv, device_id=who, device_id_type=MESH
    )


def gather_kernel(owner, pk, pv, out_k, out_v, held, send_sem, recv_sem):
    x, y, z, core = place()
    partners = [device((x + d) % GROUPS, y, z, core) for d in (1, 2, 3)]
    own = owner[lax.axis_index("br")]
    outs = (out_k, out_v)
    rows = pl.ds(pl.multiple_of(x * 64, 64), 64)
    for a, table in enumerate((pk, pv)):
        for g in range(GROUPS):
            held[a, g] = table[own, :, g * COLS : (g + 1) * COLS]
    greet(partners)
    copies = []
    for a in range(2):
        for d in (2, 1, 3):
            copies.append(
                remote(
                    held.at[a, (x + d) % GROUPS],
                    outs[a].at[rows],
                    send_sem.at[a, d - 1],
                    recv_sem.at[a, d - 1],
                    partners[d - 1],
                )
            )
            copies[-1].start()
    for a in range(2):
        outs[a][rows, :] = held[a, x]
    for copy in copies:
        copy.wait()


def gather_prefix(owners, prefix_k, prefix_v):
    own = jax.ShapeDtypeStruct((PLEN, COLS), jnp.bfloat16)
    spec = pl.BlockSpec(memory_space=VMEM)
    return pl.pallas_call(
        gather_kernel,
        out_shape=(own, own),
        in_specs=[pl.BlockSpec(memory_space=pltpu.SMEM), spec, spec],
        out_specs=(spec, spec),
        scratch_shapes=[
            VMEM((2, GROUPS, 64, COLS), jnp.bfloat16),
            pltpu.SemaphoreType.DMA((2, 3)),
            pltpu.SemaphoreType.DMA((2, 3)),
        ],
        compiler_params=pltpu.CompilerParams(
            collective_id=1, has_side_effects=True, vmem_limit_bytes=24 << 20
        ),
        name="gather_prefix",
    )(owners, prefix_k, prefix_v)


def dot(a, b):
    return jnp.dot(a, b, preferred_element_type=jnp.float32)


def dot_t(a, b):
    return lax.dot_general(a, b, (((1,), (1,)), ((), ())), preferred_element_type=jnp.float32)


def head_kernel(parents, lengths, q, k, v, o, g, pk, pv, dq, dk, dv, pdk, pdv, bias):
    @pl.when(pl.program_id(0) == 0)
    def _():
        key = lax.broadcasted_iota(jnp.int32, (TILE, TILE), 0)
        query = lax.broadcasted_iota(jnp.int32, (TILE, TILE), 1)
        reach = {}
        for b in range(BLOCKS):
            up = parents[0, b]
            for c in range(b):
                hit = (up == c).astype(jnp.int32)
                for mid in range(c + 1, b):
                    hit = hit | ((up == mid).astype(jnp.int32) & reach[mid, c])
                reach[b, c] = hit
        for c in range(BLOCKS):
            for b in range(BLOCKS):
                if b > c:
                    seen = key < reach[b, c] * lengths[0, c]
                elif b == c:
                    seen = (key < lengths[0, c]) & (key <= query)
                else:
                    seen = key < 0
                bias[c * TILE : (c + 1) * TILE, b * TILE : (b + 1) * TILE] = jnp.where(seen, 0.0, -1e30)

    scale = HS**-0.5
    row = lax.broadcasted_iota(jnp.int32, (TILE, HS), 0)
    live = [row < lengths[0, b] for b in range(BLOCKS)]
    pre_dk = pre_dv = None
    tree_dk, tree_dv = [None] * 2, [None] * 2
    pk_t = pk[...].T
    k_t = k[...].T
    for pair in range(2):
        rows = pl.ds(256 * pair, 256)
        known = 256 * (pair + 1)
        qp = q[rows, :]
        gp = jnp.concatenate(
            [jnp.where(live[b], g[b * TILE : (b + 1) * TILE, :], jnp.zeros((), g.dtype)) for b in (2 * pair, 2 * pair + 1)],
            axis=0,
        )
        spread = (gp.astype(jnp.float32) * o[rows, :].astype(jnp.float32)).T
        row_dot = jnp.sum(spread, axis=0, keepdims=True)
        s_pre = dot_t(pk[...], qp) * (scale * LOG2E)
        s_tree = dot_t(k[:known, :], qp) * (scale * LOG2E) + bias[:known, rows]
        top = jnp.maximum(jnp.max(s_pre, axis=0, keepdims=True), jnp.max(s_tree, axis=0, keepdims=True))
        e_pre = jnp.exp2(s_pre - top)
        e_tree = jnp.exp2(s_tree - top)
        total = jnp.sum(e_pre, axis=0, keepdims=True) + jnp.sum(e_tree, axis=0, keepdims=True)
        part = 1.0 / total
        a_pre = e_pre * part
        a_tree = e_tree * part
        ds_pre = (a_pre * (dot_t(pv[...], gp) - row_dot)).astype(jnp.bfloat16)
        ds_tree = (a_tree * (dot_t(v[:known, :], gp) - row_dot)).astype(jnp.bfloat16)
        a_pre = a_pre.astype(jnp.bfloat16)
        a_tree = a_tree.astype(jnp.bfloat16)
        got_dv, got_dk = dot(a_pre, gp), dot(ds_pre, qp)
        tree_v, tree_k = dot(a_tree, gp), dot(ds_tree, qp)
        dq_t = dot(pk_t, ds_pre) + dot(k_t[:, :known], ds_tree)
        dq[rows, :] = (dq_t.T * scale).astype(jnp.bfloat16)
        if pair == 0:
            pre_dk, pre_dv = got_dk, got_dv
            first_k, first_v = tree_k, tree_v
        else:
            pdk[...] = ((pre_dk + got_dk) * scale).astype(jnp.bfloat16)
            pdv[...] = (pre_dv + got_dv).astype(jnp.bfloat16)
            dk[:256, :] = ((first_k + tree_k[:256]) * scale).astype(jnp.bfloat16)
            dv[:256, :] = (first_v + tree_v[:256]).astype(jnp.bfloat16)
            dk[256:, :] = (tree_k[256:] * scale).astype(jnp.bfloat16)
            dv[256:, :] = tree_v[256:].astype(jnp.bfloat16)


def heads(parents, lengths, q, k, v, o, g, pk, pv):
    tree = pl.BlockSpec((ROWS, HS), lambda h: (0, h))
    pre = pl.BlockSpec((PLEN, HS), lambda h: (0, h))
    table = pl.BlockSpec(memory_space=pltpu.SMEM)
    big = jax.ShapeDtypeStruct((ROWS, COLS), jnp.bfloat16)
    small = jax.ShapeDtypeStruct((PLEN, COLS), jnp.bfloat16)
    return pl.pallas_call(
        head_kernel,
        grid=(HEADS,),
        out_shape=(big, big, big, small, small),
        in_specs=[table, table, tree, tree, tree, tree, tree, pre, pre],
        out_specs=(tree, tree, tree, pre, pre),
        scratch_shapes=[VMEM((ROWS, ROWS), jnp.float32)],
        compiler_params=pltpu.CompilerParams(vmem_limit_bytes=32 << 20),
        name="head_grads",
    )(parents, lengths, q, k, v, o, g, pk, pv)


def f32(value):
    return value.astype(jnp.float32)


def bf16(value):
    return value.astype(jnp.bfloat16)


def reduce_kernel(owner, dkp, dvp, out_k, out_v, *scratch):
    x, y, z, core = place()
    (other, part0, part1, line0, line1, got_y0, got_y1, got_z0, got_z1, all0, all1, swap0, swap1,
     core_send, core_recv, y_send, y_recv, z_send, z_recv, x_send, x_recv,
     ay_send, ay_recv, az_send, az_recv, end_send, end_recv) = scratch
    mate = device(x, y, z, 1 - core)
    y_peers = [device(x, (y + d) % NY, z, core) for d in range(1, NY)]
    z_peers = [device(x, y, (z + d) % NZ, core) for d in range(1, NZ)]
    x_peers = [device((x + d) % GROUPS, y, z, core) for d in range(1, GROUPS)]
    greet([mate] + y_peers + z_peers + x_peers)
    br = lax.axis_index("br")
    mine = owner[br]
    its = owner[br + 1 - 2 * core]
    outs = (out_k, out_v)
    sums = (dkp, dvp)

    def one_core(c, part, line, got_y, got_z, full):
        width, start = WIDTHS[c], STARTS[c]
        other_width, other_start = WIDTHS[1 - c], STARTS[1 - c]
        first = []
        for a in range(2):
            copy = remote(
                sums[a].at[:, pl.ds(other_start, 2 * other_width)],
                other.at[a, :, pl.ds(0, 2 * other_width)],
                core_send.at[a],
                core_recv.at[a],
                mate,
            )
            copy.start()
            back = remote(
                sums[a].at[:, pl.ds(start, 2 * width)],
                other.at[a, :, pl.ds(0, 2 * width)],
                core_send.at[a],
                core_recv.at[a],
                mate,
            )
            first.append((copy, back))
        weights = [
            ((mine == p).astype(jnp.float32), (its == p).astype(jnp.float32)) for p in range(PROMPTS)
        ]
        for a in range(2):
            first[a][0].wait_send()
            first[a][1].wait_recv()

            @pl.loop(0, 16)
            def _(tile, a=a):
                to, rt = tile // 4, tile % 4
                rows = pl.ds(pl.multiple_of(tile * 16, 16), 16)
                for half in range(2):
                    own = f32(sums[a][rows, start + half * width : start + (half + 1) * width])
                    its_rows = f32(other[a, rows, half * width : (half + 1) * width])
                    for p in range(PROMPTS):
                        part[2 * a + half, 4 * p + rt, to] = bf16(weights[p][0] * own + weights[p][1] * its_rows)

        def spread(axis_peers, me, count, block, landing, sends, recvs):
            copies = []
            for d in range(1, count):
                copy = remote(block((me + d) % count), landing.at[d - 1], sends.at[d - 1], recvs.at[d - 1], axis_peers[d - 1])
                copy.start()
                copies.append(copy)
            for copy in copies:
                copy.wait()

        if c == 0:
            spread(y_peers, y, NY, lambda t: part.at[t], got_y, y_send, y_recv)

            @pl.loop(0, NZ * GROUPS)
            def _(i):
                a, b = i // GROUPS, i % GROUPS
                total = f32(part[y, a, b])
                for d in range(NY - 1):
                    total += f32(got_y[d, a, b])
                line[a, b] = bf16(total)

            spread(z_peers, z, NZ, lambda t: line.at[t], got_z, z_send, z_recv)

            @pl.loop(0, GROUPS)
            def _(b):
                total = f32(line[z, b])
                for d in range(NZ - 1):
                    total += f32(got_z[d, b])
                line[z, b] = bf16(total)

            block = line.at[z]
        else:
            spread(z_peers, z, NZ, lambda t: part.at[:, t], got_z, z_send, z_recv)

            @pl.loop(0, NY * GROUPS)
            def _(i):
                a, b = i // GROUPS, i % GROUPS
                total = f32(part[a, z, b])
                for d in range(NZ - 1):
                    total += f32(got_z[d, a, b])
                line[a, b] = bf16(total)

            spread(y_peers, y, NY, lambda t: line.at[t], got_y, y_send, y_recv)

            @pl.loop(0, GROUPS)
            def _(b):
                total = f32(line[y, b])
                for d in range(NY - 1):
                    total += f32(got_y[d, b])
                line[y, b] = bf16(total)

            block = line.at[y]
        full[y, z, x] = block[x]
        copies = []
        for d in range(1, GROUPS):
            copy = remote(
                block.at[(x + d) % GROUPS], full.at[y, z, x], x_send.at[d - 1], x_recv.at[d - 1], x_peers[d - 1]
            )
            copy.start()
            copies.append(copy)
        for copy in copies:
            copy.wait()

        def share(axis_peers, ref, sends, recvs):
            copies = []
            for d in range(len(axis_peers)):
                copy = remote(ref, ref, sends.at[d], recvs.at[d], axis_peers[d])
                copy.start()
                copies.append(copy)
            for copy in copies:
                copy.wait()

        if c == 0:
            share(z_peers, full.at[y, z], az_send, az_recv)
            share(y_peers, full.at[y], ay_send, ay_recv)
        else:
            share(y_peers, full.at[y, z], ay_send, ay_recv)
            share(z_peers, full.at[:, z], az_send, az_recv)

    @pl.when(core == 0)
    def _():
        one_core(0, part0, line0, got_y0, got_z0, all0)
        copy = remote(all0, swap0, end_send.at[0], end_recv.at[0], mate)
        back = remote(all1, swap1, end_send.at[1], end_recv.at[1], mate)
        copy.start()
        copy.wait_send()
        back.wait_recv()

    @pl.when(core == 1)
    def _():
        one_core(1, part1, line1, got_y1, got_z1, all1)
        copy = remote(all1, swap1, end_send.at[1], end_recv.at[1], mate)
        back = remote(all0, swap0, end_send.at[0], end_recv.at[0], mate)
        copy.start()
        copy.wait_send()
        back.wait_recv()

    def place_all(sources):
        @pl.loop(0, NZ)
        def _(t):
            p, rt = t // 4, t % 4
            rows = pl.ds(pl.multiple_of(rt * 16, 16), 16)
            for c in range(2):
                for yy in range(NY):
                    for xx in range(GROUPS):
                        at = xx * COLS + STARTS[c] + (yy % 2) * WIDTHS[c]
                        outs[yy // 2][p, rows, at : at + WIDTHS[c]] = sources[c][yy, t, xx]

    @pl.when(core == 0)
    def _():
        place_all((all0, swap1))

    @pl.when(core == 1)
    def _():
        place_all((swap0, all1))


def reduce_prefix(owners, dkp, dvp):
    out = jax.ShapeDtypeStruct((PROMPTS, 64, GROUPS * COLS), jnp.bfloat16)
    spec = pl.BlockSpec(memory_space=VMEM)
    w0, w1 = WIDTHS
    dma = pltpu.SemaphoreType.DMA

    def buf(*shape):
        return VMEM(shape, jnp.bfloat16)

    return pl.pallas_call(
        reduce_kernel,
        out_shape=(out, out),
        in_specs=[pl.BlockSpec(memory_space=pltpu.SMEM), spec, spec],
        out_specs=(spec, spec),
        scratch_shapes=[
            buf(2, PLEN, 768),
            buf(NY, NZ, GROUPS, 16, w0),
            buf(NY, NZ, GROUPS, 16, w1),
            buf(NZ, GROUPS, 16, w0),
            buf(NY, GROUPS, 16, w1),
            buf(NY - 1, NZ, GROUPS, 16, w0),
            buf(NY - 1, GROUPS, 16, w1),
            buf(NZ - 1, GROUPS, 16, w0),
            buf(NZ - 1, NY, GROUPS, 16, w1),
            buf(NY, NZ, GROUPS, 16, w0),
            buf(NY, NZ, GROUPS, 16, w1),
            buf(NY, NZ, GROUPS, 16, w0),
            buf(NY, NZ, GROUPS, 16, w1),
            dma((2,)),
            dma((2,)),
            dma((NY - 1,)),
            dma((NY - 1,)),
            dma((NZ - 1,)),
            dma((NZ - 1,)),
            dma((GROUPS - 1,)),
            dma((GROUPS - 1,)),
            dma((NY - 1,)),
            dma((NY - 1,)),
            dma((NZ - 1,)),
            dma((NZ - 1,)),
            dma((2,)),
            dma((2,)),
        ],
        compiler_params=pltpu.CompilerParams(
            collective_id=2, has_side_effects=True, vmem_limit_bytes=40 << 20
        ),
        name="reduce_prefix",
    )(owners, dkp, dvp)


def per_device(q, k, v, o, g, prefix_k, prefix_v, parents, lengths, prompt_of):
    owners = prompt_of[:, 0]
    pk, pv = gather_prefix(owners, prefix_k, prefix_v)
    dq, dk, dv, dkp, dvp = heads(parents, lengths, q, k, v, o, g, pk, pv)
    prefix_dk, prefix_dv = reduce_prefix(owners, dkp, dvp)
    return dq, dk, dv, prefix_dk, prefix_dv


def solution(mesh):
    split = P("br", "hd")
    held = P(None, "hd", None)
    return jax.shard_map(
        per_device,
        mesh=mesh,
        in_specs=(split,) * 5 + (held, held, P("br", None), P("br", None), P()),
        out_specs=(split,) * 3 + (held, held),
        check_vma=False,
    )
```

time: 492 us -> 116 us (0.24); the launches traced: 486 us -> 116 us
  blocking collectives: 296 us -> 0 us
  Pallas kernels: 0 us -> 105 us
  matrix products: 85.6 us -> 0 us
  waiting for transfers between devices: 30 us -> 0 us
  other arithmetic: 26.2 us -> 0 us
  local copies, waits for them, and re-layouts: 32.8 us -> 9.36 us
  starting transfers between devices: 12.7 us -> 0 us
    psum x1 -> x0, blocking collectives: 296 us -> none  [per_device(): summed = lax.psum(slab[:, :, None, :] * selected[None, None, :, None], 'br')]
    pallas_call x0 -> x3, Pallas kernels: none -> 105 us  [the longest x1 65.5 us: reduce_prefix(): pl.pallas_call(reduce_kernel, out_shape=(out, out), in_specs=[pl.BlockSpe...]
    dot_general x50 -> x0, matrix products: 85.6 us -> none  [the longest x10 24.2 us: head_grads(): jnp.dot(attention_low.T, kept_grad, preferred_element_type=jnp.float32)]
    all_to_all x3 -> x0, waiting for transfers between devices: 30 us -> none  [the longest x1 20.1 us: per_device(): lax.all_to_all(arranged, 'hd', split_axis=0, concat_axis=4, tiled=True)]
    reduce_sum x20 -> x0, other arithmetic: 16.2 us -> none  [the longest x10 12 us: head_grads(): jnp.sum(kept_grad.astype(jnp.float32) * output.astype(jnp.float32), axis=...]
    all_to_all x3 -> x0, starting transfers between devices: 12.7 us -> none  [the longest x1 4.84 us: per_device(): lax.all_to_all(own_slab(prefix_k), 'hd', split_axis=1, concat_axis=0, til...]
    reshape x6 -> x0, local copies, waits for them, and re-layouts: 8.99 us -> none  [the longest x1 4.54 us: per_device(): merged = spread.reshape(own_rows, 2, prompts, full_width)]
    unnamed x7 -> x24, local copies, waits for them, and re-layouts: 0.8 us -> 9.36 us
  transfers between devices with their start and end apart: 3 -> 0, of which waited for: 3 -> 0; matrix products, arithmetic and copies ran while one was open for 3% -> 0% of each run, Pallas kernels for 0% -> 0%
where the time goes in v1:
time: 116 us
  Pallas kernels  105 us (91%)
  local copies, waits for them, and re-layouts  9.36 us (8%)
    pallas_call x1, Pallas kernels, reduce_prefix(): pl.pallas_call(reduce_kernel, out_shape=(out, out), in_specs=[pl.BlockSpe...  65.5 us
    pallas_call x1, Pallas kernels, gather_prefix(): pl.pallas_call(gather_kernel, out_shape=(own, own), in_specs=[pl.BlockSpe...  20.4 us
    pallas_call x1, Pallas kernels, heads(): pl.pallas_call(head_kernel, grid=(HEADS,), out_shape=(big, big, big, smal...  19.5 us
    unnamed x24, local copies, waits for them, and re-layouts  9.36 us

profile of v1, /device:TPU:1, one launch (start us, length us, event | category | flops | bytes accessed | tf_op | source)
XLA Modules:
  0.0 115.5 jit_solution(9878689254008619925)
XLA Ops:
  0.6 0.0 copy-start
  0.6 1.3 %copy-done = bf16[2,64,5120]{2,1,0:T(8,128)(2,1)S(1)} copy-done((bf16[2,64,5120]{2,1,0:T(8,128)(2,1)S(1)}, bf16[2,64,5120]{2,1,0:T(8,128)(2,1)}, u32[]{:S(2)}) %copy-start) | copy-done | bytes 1310744
  2.0 0.0 copy-start.1
  2.0 1.3 %copy-done.1 = bf16[2,64,5120]{2,1,0:T(8,128)(2,1)S(1)} copy-done((bf16[2,64,5120]{2,1,0:T(8,128)(2,1)S(1)}, bf16[2,64,5120]{2,1,0:T(8,128)(2,1)}, u32[]{:S(2)}) %copy-start.1) | copy-done | bytes 1310744
  3.3 0.0 copy-start.7
  3.3 0.7 copy-done.7
  3.9 0.0 copy-start.2
  3.9 0.0 copy-start.9
  3.9 0.0 copy-start.10
  3.9 20.4 %gather_prefix.1 = (bf16[256,1280]{1,0:T(8,128)(2,1)S(1)}, bf16[256,1280]{1,0:T(8,128)(2,1)S(1)}) custom-call(s32[64]{0:T(128)S(1)} %bitcast.1, bf16[2,64,5120]{2,1,0:T(8,128)(2,1)S(1)} %copy-done, bf16[2,64,5120]{2,1,0:T(8,128)(2,1)S(1)} %copy-done.1), custom_call_target="tpu_custom_call" | custom-call | tf_op jit(solution)/shard_map/gather_prefix/pallas_call | solution.py:85
  24.4 0.0 copy-done.2
  24.4 0.0 copy-done.3
  24.4 0.0 copy-done.9
  24.4 0.0 copy-done.10
  24.4 0.0 copy-start.4
  24.4 1.3 %copy-done.4 = bf16[512,1280]{1,0:T(8,128)(2,1)S(1)} copy-done((bf16[512,1280]{1,0:T(8,128)(2,1)S(1)}, bf16[512,1280]{1,0:T(8,128)(2,1)}, u32[]{:S(2)}) %copy-start.4) | copy-done | bytes 1310744
  25.7 0.0 copy-start.5
  25.7 1.3 %copy-done.5 = bf16[512,1280]{1,0:T(8,128)(2,1)S(1)} copy-done((bf16[512,1280]{1,0:T(8,128)(2,1)S(1)}, bf16[512,1280]{1,0:T(8,128)(2,1)}, u32[]{:S(2)}) %copy-start.5) | copy-done | bytes 1310744
  27.1 1.3 %copy-done.6 = bf16[512,1280]{1,0:T(8,128)(2,1)S(1)} copy-done((bf16[512,1280]{1,0:T(8,128)(2,1)S(1)}, bf16[512,1280]{1,0:T(8,128)(2,1)}, u32[]{:S(2)}) %copy-start.6) | copy-done | bytes 1310744
  28.4 19.5 %head_grads.1 = (bf16[512,1280]{1,0:T(8,128)(2,1)}, bf16[512,1280]{1,0:T(8,128)(2,1)}, bf16[512,1280]{1,0:T(8,128)(2,1)}, bf16[256,1280]{1,0:T(8,128)(2,1)S(1)}, bf16[256,1280]{1,0:T(8,128)(2,1)S(1)}) custom-call(s32[1,4]{1,0:T(1,128)S(1)} %copy-done.9, s32[1,4]{1,0:T(1,128)S(1)} %copy-done.10, bf16[512,1280]{1,0:T(8,128)(2,1)S(1)} %copy-done.2, ...), custom_call_target="tpu_custom_call" | custom-call | tf_op jit(solution)/shard_map/head_grads/pallas_call | solution.py:185
  47.9 0.0 copy-done.8
  47.9 65.5 %reduce_prefix.1 = (bf16[2,64,5120]{2,1,0:T(8,128)(2,1)S(1)}, bf16[2,64,5120]{2,1,0:T(8,128)(2,1)S(1)}) custom-call(s32[64]{0:T(128)S(1)} %bitcast.2, bf16[256,1280]{1,0:T(8,128)(2,1)S(1)} %get-tuple-element.19.dkp, bf16[256,1280]{1,0:T(8,128)(2,1)S(1)} %get-tuple-element.20.dvp), custom_call_target="tpu_custom_call" | custom-call | tf_op jit(solution)/shard_map/reduce_prefix/pallas_call | solution.py:384
  113.4 1.1 copy.17
  114.5 1.1 copy.18
  (3 shorter events, 0.0 us)
Async XLA Ops:
  0.6 1.3 %copy-start = (bf16[2,64,5120]{2,1,0:T(8,128)(2,1)S(1)}, bf16[2,64,5120]{2,1,0:T(8,128)(2,1)}, u32[]{:S(2)}) copy-start(bf16[2,64,5120]{2,1,0:T(8,128)(2,1)} %pk.1) | copy-start | bytes 3932164
  2.0 1.3 %copy-start.1 = (bf16[2,64,5120]{2,1,0:T(8,128)(2,1)S(1)}, bf16[2,64,5120]{2,1,0:T(8,128)(2,1)}, u32[]{:S(2)}) copy-start(bf16[2,64,5120]{2,1,0:T(8,128)(2,1)} %pv.1) | copy-start | bytes 3932164
  3.3 0.7 copy-start.7
  3.9 20.4 %copy-start.2 = (bf16[512,1280]{1,0:T(8,128)(2,1)S(1)}, bf16[512,1280]{1,0:T(8,128)(2,1)}, u32[]{:S(2)}) copy-start(bf16[512,1280]{1,0:T(8,128)(2,1)} %q.1) | copy-start | bytes 3932164
  3.9 20.5 %copy-start.3 = (bf16[512,1280]{1,0:T(8,128)(2,1)S(1)}, bf16[512,1280]{1,0:T(8,128)(2,1)}, u32[]{:S(2)}) copy-start(bf16[512,1280]{1,0:T(8,128)(2,1)} %k.1) | copy-start | bytes 3932164
  3.9 20.5 %copy-start.9 = (s32[1,4]{1,0:T(1,128)S(1)}, s32[1,4]{1,0:T(1,128)}, u32[]{:S(2)}) copy-start(s32[1,4]{1,0:T(1,128)} %parents.1) | copy-start | bytes 52
  3.9 20.5 %copy-start.10 = (s32[1,4]{1,0:T(1,128)S(1)}, s32[1,4]{1,0:T(1,128)}, u32[]{:S(2)}) copy-start(s32[1,4]{1,0:T(1,128)} %lengths.1) | copy-start | bytes 52
  24.4 1.3 %copy-start.4 = (bf16[512,1280]{1,0:T(8,128)(2,1)S(1)}, bf16[512,1280]{1,0:T(8,128)(2,1)}, u32[]{:S(2)}) copy-start(bf16[512,1280]{1,0:T(8,128)(2,1)} %v.1) | copy-start | bytes 3932164
  25.7 1.3 %copy-start.5 = (bf16[512,1280]{1,0:T(8,128)(2,1)S(1)}, bf16[512,1280]{1,0:T(8,128)(2,1)}, u32[]{:S(2)}) copy-start(bf16[512,1280]{1,0:T(8,128)(2,1)} %o.1) | copy-start | bytes 3932164
  27.0 1.3 %copy-start.6 = (bf16[512,1280]{1,0:T(8,128)(2,1)S(1)}, bf16[512,1280]{1,0:T(8,128)(2,1)}, u32[]{:S(2)}) copy-start(bf16[512,1280]{1,0:T(8,128)(2,1)} %g.1) | copy-start | bytes 3932164
  28.4 19.5 %copy-start.8 = (s32[64,1]{0,1:T(1,128)S(1)}, s32[64,1]{0,1:T(1,128)}, u32[]{:S(2)}) copy-start(s32[64,1]{0,1:T(1,128)} %param.19) | copy-start | bytes 772

commit v2 on v0

v2 whole, which is shorter than its diff:
```python
import jax
import jax.numpy as jnp
from jax import lax
from jax.experimental import pallas as pl
from jax.experimental.pallas import tpu as pltpu
from jax.sharding import PartitionSpec as P

HS = 128
TILE = 128
BLOCKS = 4
PLEN = 256
PROMPTS = 2
ROWS = 512
HEADS = 10
COLS = 1280
GROUPS = 4
NY = 4
NZ = 8
BATCHES = HEADS // 2
OWN_ROWS = PLEN // GROUPS
SCALE = HS**-0.5
LOG2E = 1.4426950408889634
MESH = pl.DeviceIdType.MESH
VMEM = pltpu.VMEM
BF16 = jnp.bfloat16
F32 = jnp.float32
LAGS = (2, 8, 14, 17, 23, 28, 30)


def place():
    br = lax.axis_index("br")
    return lax.axis_index("hd"), (br // 2) % NY, br // (2 * NY), br % 2


def device(x, y, z, core):
    return ((z * NY + y) * 2 + core, x)


def remote(src, dst, send, recv, who):
    return pltpu.make_async_remote_copy(
        src_ref=src, dst_ref=dst, send_sem=send, recv_sem=recv, device_id=who, device_id_type=MESH
    )


def dot(a, b):
    return jnp.dot(a, b, preferred_element_type=F32)


def dot_t(a, b):
    return lax.dot_general(a, b, (((1,), (1,)), ((), ())), preferred_element_type=F32)


def cols_of(h):
    return pl.ds(pl.multiple_of(h * HS, HS), HS)


def fill_bias(parents, lengths, bias):
    key = lax.broadcasted_iota(jnp.int32, (TILE, TILE), 0)
    query = lax.broadcasted_iota(jnp.int32, (TILE, TILE), 1)
    reach = {}
    for b in range(BLOCKS):
        up = parents[0, b]
        for c in range(b):
            hit = (up == c).astype(jnp.int32)
            for mid in range(c + 1, b):
                hit = hit | ((up == mid).astype(jnp.int32) & reach[mid, c])
            reach[b, c] = hit
    for c in range(BLOCKS):
        for b in range(BLOCKS):
            if b > c:
                seen = key < reach[b, c] * lengths[0, c]
            elif b == c:
                seen = (key < lengths[0, c]) & (key <= query)
            else:
                seen = key < 0
            bias[c * TILE : (c + 1) * TILE, b * TILE : (b + 1) * TILE] = jnp.where(seen, 0.0, -1e30)


def kernel(
    parents, lengths, owner, q_hbm, k_hbm, v_hbm, o_hbm, g_hbm, pk_hbm, pv_hbm,
    dq, dk, dv, out_k, out_v,
    q, k, v, o, g, table_k, table_v, held, pre, bias, e_tree, g_tree, stats, ds_pre,
    part, got1, line, got2, fin, full,
    load_sem, pre_send, pre_recv, s1_send, s1_recv, s2_send, s2_recv, s3_send, s3_recv,
    s4_send, s4_recv, s5_send, s5_recv, s6_send, s6_recv,
):
    x, y, z, core = place()
    mate = device(x, y, z, 1 - core)
    br = lax.axis_index("br")

    barrier = pltpu.get_barrier_semaphore()
    partners = [mate]
    partners += [device((x + d) % GROUPS, y, z, core) for d in range(1, GROUPS)]
    partners += [device(x, (y + d) % NY, z, c) for d in range(1, NY) for c in range(2)]
    partners += [device(x, y, (z + d) % NZ, core) for d in range(1, NZ)]
    for who in partners:
        pl.semaphore_signal(barrier, inc=1, device_id=who, device_id_type=MESH)

    loads = []
    pairs = ((pk_hbm, table_k), (pv_hbm, table_v), (q_hbm, q), (k_hbm, k), (g_hbm, g), (o_hbm, o), (v_hbm, v))
    for i, (src, dst) in enumerate(pairs):
        loads.append(pltpu.make_async_copy(src, dst, load_sem.at[i]))
        loads[-1].start()

    mine = owner[br]
    fill_bias(parents, lengths, bias)
    for a, table in enumerate((table_k, table_v)):
        loads[a].wait()
        for to in range(GROUPS):
            held[a, to] = table[mine, :, to * COLS : (to + 1) * COLS]
    pl.semaphore_wait(barrier, len(partners))

    own_rows = pl.ds(pl.multiple_of(x * OWN_ROWS, OWN_ROWS), OWN_ROWS)
    gathers = []
    for a in range(2):
        for d in range(1, GROUPS):
            gathers.append(
                remote(
                    held.at[a, (x + d) % GROUPS], pre.at[a, own_rows], pre_send.at[a, d - 1], pre_recv.at[a, d - 1],
                    device((x + d) % GROUPS, y, z, core),
                )
            )
            gathers[-1].start()
    for a in range(2):
        pre[a, own_rows] = held[a, x]
    for load in loads[2:]:
        load.wait()

    row = lax.broadcasted_iota(jnp.int32, (TILE, HS), 0)

    @pl.loop(0, HEADS)
    def _(h):
        cols = cols_of(h)
        for pair in range(2):
            rows = pl.ds(256 * pair, 256)
            known = 256 * (pair + 1)
            base = 256 * pair
            qp = q[rows, cols]
            for b in (2 * pair, 2 * pair + 1):
                at = pl.ds(b * TILE, TILE)
                g[at, cols] = jnp.where(row < lengths[0, b], g[at, cols], jnp.zeros((), BF16))
            gp = g[rows, cols]
            row_dot = jnp.sum((gp.astype(F32) * o[rows, cols].astype(F32)).T, axis=0, keepdims=True)
            s = dot_t(k[:known, cols], qp) * (SCALE * LOG2E) + bias[:known, rows]
            top = jnp.max(s, axis=0, keepdims=True)
            e = jnp.exp2(s - top)
            stats[h, pair, 0:1] = top
            stats[h, pair, 1:2] = jnp.sum(e, axis=0, keepdims=True)
            stats[h, pair, 2:3] = row_dot
            e_tree[h, base : base + known] = e
            g_tree[h, base : base + known] = e * (dot_t(v[:known, cols], gp) - row_dot)

    for copy in gathers:
        copy.wait()

    def prompt_part(h):
        cols = cols_of(h)
        key_sum = value_sum = None
        for pair in range(2):
            rows = pl.ds(256 * pair, 256)
            qp, gp = q[rows, cols], g[rows, cols]
            top_tree, sum_tree, row_dot = stats[h, pair, 0:1], stats[h, pair, 1:2], stats[h, pair, 2:3]
            s = dot_t(pre[0, :, cols], qp) * (SCALE * LOG2E)
            top = jnp.maximum(jnp.max(s, axis=0, keepdims=True), top_tree)
            e = jnp.exp2(s - top)
            carry = jnp.exp2(top_tree - top)
            share = 1.0 / (jnp.sum(e, axis=0, keepdims=True) + sum_tree * carry)
            stats[h, pair, 3:4] = carry * share
            att = e * share
            ds = (att * (dot_t(pre[1, :, cols], gp) - row_dot)).astype(BF16)
            ds_pre[h, pair] = ds
            got_k, got_v = dot(ds, qp), dot(att.astype(BF16), gp)
            key_sum = got_k if pair == 0 else key_sum + got_k
            value_sum = got_v if pair == 0 else value_sum + got_v
        j, hp = h // 2, h % 2
        part[j, 2 * hp] = (key_sum * SCALE).astype(BF16)
        part[j, 2 * hp + 1] = value_sum.astype(BF16)

    def tree_part(h):
        cols = cols_of(h)
        keys, pre_keys = k[:, cols].T, pre[0, :, cols].T
        first_k = first_v = None
        for pair in range(2):
            rows = pl.ds(256 * pair, 256)
            known = 256 * (pair + 1)
            base = 256 * pair
            qp, gp = q[rows, cols], g[rows, cols]
            factor = stats[h, pair, 3:4]
            att = (e_tree[h, base : base + known] * factor).astype(BF16)
            ds = (g_tree[h, base : base + known] * factor).astype(BF16)
            got_k, got_v = dot(ds, qp), dot(att, gp)
            dq_t = dot(pre_keys, ds_pre[h, pair]) + dot(keys[:, :known], ds)
            dq[rows, cols] = (dq_t.T * SCALE).astype(BF16)
            if pair == 0:
                first_k, first_v = got_k, got_v
            else:
                dk[:256, cols] = ((first_k + got_k[:256]) * SCALE).astype(BF16)
                dv[:256, cols] = (first_v + got_v[:256]).astype(BF16)
                dk[256:, cols] = (got_k[256:] * SCALE).astype(BF16)
                dv[256:, cols] = got_v[256:].astype(BF16)

    def far1(j, d):
        to = (y + d) % NY
        own = j % 2
        off = (core + own) % 2
        return remote(
            part.at[j, to], got1.at[j, 2 * d + off], s1_send.at[j, d], s1_recv.at[j, 2 * d + off], device(x, to, z, own)
        )

    def land1(j, slot):
        return remote(part.at[j, 0], got1.at[j, slot], s1_send.at[j, 0], s1_recv.at[j, slot], mate)

    def far2(j, d):
        to = (z + d) % NZ
        return remote(line.at[j, to], got2.at[j, d - 1], s2_send.at[j, d - 1], s2_recv.at[j, d - 1], device(x, y, to, core))

    def far3(j, d):
        to = (x + d) % GROUPS
        return remote(
            fin.at[j, to], full.at[j, y, z, x], s3_send.at[j, d - 1], s3_recv.at[j, d - 1], device(to, y, z, core)
        )

    def far4(j, d):
        ref = full.at[j, y, z]
        return remote(ref, ref, s4_send.at[j, d - 1], s4_recv.at[j, d - 1], device(x, y, (z + d) % NZ, core))

    def far5(j, d):
        ref = full.at[j, y]
        return remote(ref, ref, s5_send.at[j, d - 1], s5_recv.at[j, d - 1], device(x, (y + d) % NY, z, core))

    def far6(j, d):
        ref = full.at[j, (y + NY - d) % NY]
        return remote(ref, ref, s6_send.at[j, d], s6_recv.at[j, d], mate)

    def send1(j):
        for d in (2, 1, 3):
            far1(j, d).start()

        @pl.when(core == j % 2)
        def _():
            got1[j, 0] = part[j, y]

        @pl.when(core != j % 2)
        def _():
            far1(j, 0).start()

    def sum1(j):
        for slot in range(1, 2 * NY):
            land1(j, slot).wait_recv()
        weights = []
        for slot in range(2 * NY):
            d, off = slot // 2, slot % 2
            whose = owner[(z * NY + (y + NY - d) % NY) * 2 + (core + off) % 2]
            weights.append([(whose == p).astype(F32) for p in range(PROMPTS)])

        @pl.loop(0, 16)
        def _(tile):
            to, rt = tile // 4, tile % 4
            rows = pl.ds(pl.multiple_of(tile * 16, 16), 16)
            sums = [None] * PROMPTS
            for slot in range(2 * NY):
                term = got1[j, slot, rows].astype(F32)
                for p in range(PROMPTS):
                    scaled = weights[slot][p] * term
                    sums[p] = scaled if slot == 0 else sums[p] + scaled
            for p in range(PROMPTS):
                line[j, 4 * p + rt, to] = sums[p].astype(BF16)

        for d in (4, 3, 5, 2, 6, 1, 7):
            far2(j, d).start()

    def sum2(j):
        for d in range(1, NZ):
            far2(j, d).wait()
        for to in range(GROUPS):
            total = line[j, z, to].astype(F32)
            for d in range(1, NZ):
                total += got2[j, d - 1, to].astype(F32)
            fin[j, to] = total.astype(BF16)
        for d in (2, 1, 3):
            far3(j, d).start()
        full[j, y, z, x] = fin[j, x]

    def share3(j):
        for d in range(1, GROUPS):
            far3(j, d).wait()
        for d in (4, 3, 5, 2, 6, 1, 7):
            far4(j, d).start()

    def share4(j):
        for d in range(1, NZ):
            far4(j, d).wait()
        for d in (2, 1, 3):
            far5(j, d).start()
        far6(j, 0).start()

    def share5(j):
        for d in range(1, NY):
            far5(j, d).wait()
            far6(j, d).start()

    def finish(j):
        @pl.when(core != j % 2)
        def _():
            for d in range(NY):
                far6(j, d).wait_recv()

        @pl.loop(0, NZ)
        def _(t):
            p, rt = t // 4, t % 4
            rows = pl.ds(pl.multiple_of(rt * 16, 16), 16)
            for hp in range(2):
                for a, out in enumerate((out_k, out_v)):
                    for xx in range(GROUPS):
                        at = pl.ds(pl.multiple_of((xx * HEADS + 2 * j + hp) * HS, HS), HS)
                        out[p, rows, at] = full[j, 2 * hp + a, t, xx]

    def stage(step, lag, whole, work):
        j = (step - lag) // 2
        due = (step >= lag) & (step < lag + 2 * BATCHES) & ((step - lag) % 2 == 0)
        if not whole:
            due = due & (core == j % 2)

        @pl.when(due)
        def _():
            work(j)

    @pl.loop(0, 2 * BATCHES + LAGS[-1])
    def _(step):
        @pl.when(step < HEADS)
        def _():
            prompt_part(step)

        @pl.when((step >= HEADS) & (step < 2 * HEADS))
        def _():
            tree_part(step - HEADS)

        stage(step + 1, LAGS[0], True, send1)
        stage(step, LAGS[1], False, sum1)
        stage(step, LAGS[2], False, sum2)
        stage(step, LAGS[3], False, share3)
        stage(step, LAGS[4], False, share4)
        stage(step, LAGS[5], False, share5)
        stage(step, LAGS[6], True, finish)

    @pl.loop(0, BATCHES)
    def _(j):
        for d in range(1, NY):
            far1(j, d).wait_send()

        @pl.when(core != j % 2)
        def _():
            far1(j, 0).wait_send()

        @pl.when(core == j % 2)
        def _():
            for d in range(NY):
                far6(j, d).wait_send()


def fused(parents, lengths, owners, q, k, v, o, g, prefix_k, prefix_v):
    smem = pl.BlockSpec(memory_space=pltpu.SMEM)
    hbm = pl.BlockSpec(memory_space=pltpu.HBM)
    vmem = pl.BlockSpec(memory_space=VMEM)
    big = jax.ShapeDtypeStruct((ROWS, COLS), BF16)
    small = jax.ShapeDtypeStruct((PROMPTS, OWN_ROWS, GROUPS * COLS), BF16)
    sem = pltpu.SemaphoreType.DMA

    def pair(*shape):
        return [sem(shape), sem(shape)]

    return pl.pallas_call(
        kernel,
        out_shape=(big, big, big, small, small),
        in_specs=[smem] * 3 + [hbm] * 7,
        out_specs=(vmem,) * 5,
        scratch_shapes=[VMEM((ROWS, COLS), BF16)] * 5
        + [VMEM((PROMPTS, OWN_ROWS, GROUPS * COLS), BF16)] * 2
        + [
            VMEM((2, GROUPS, OWN_ROWS, COLS), BF16),
            VMEM((2, PLEN, COLS), BF16),
            VMEM((ROWS, ROWS), F32),
            VMEM((HEADS, 768, 256), F32),
            VMEM((HEADS, 768, 256), F32),
            VMEM((HEADS, 2, 8, 256), F32),
            VMEM((HEADS, 2, PLEN, 256), BF16),
            VMEM((BATCHES, NY, PLEN, HS), BF16),
            VMEM((BATCHES, 2 * NY, PLEN, HS), BF16),
            VMEM((BATCHES, NZ, GROUPS, 16, HS), BF16),
            VMEM((BATCHES, NZ - 1, GROUPS, 16, HS), BF16),
            VMEM((BATCHES, GROUPS, 16, HS), BF16),
            VMEM((BATCHES, NY, NZ, GROUPS, 16, HS), BF16),
            sem((7,)),
        ]
        + pair(2, GROUPS - 1)
        + [sem((BATCHES, NY)), sem((BATCHES, 2 * NY))]
        + pair(BATCHES, NZ - 1)
        + pair(BATCHES, GROUPS - 1)
        + pair(BATCHES, NZ - 1)
        + pair(BATCHES, NY - 1)
        + pair(BATCHES, NY),
        compiler_params=pltpu.CompilerParams(
            collective_id=1, has_side_effects=True, vmem_limit_bytes=44 << 20
        ),
        name="tree_grads",
    )(parents, lengths, owners, q, k, v, o, g, prefix_k, prefix_v)


def per_device(q, k, v, o, g, prefix_k, prefix_v, parents, lengths, prompt_of):
    return fused(parents, lengths, prompt_of[:, 0], q, k, v, o, g, prefix_k, prefix_v)


def solution(mesh):
    split = P("br", "hd")
    held = P(None, "hd", None)
    return jax.shard_map(
        per_device,
        mesh=mesh,
        in_specs=(split,) * 5 + (held, held, P("br", None), P("br", None), P()),
        out_specs=(split,) * 3 + (held, held),
        check_vma=False,
    )
```

time: 492 us -> 85 us (0.17); the launches traced: 486 us -> 84.8 us
  blocking collectives: 296 us -> 0 us
  matrix products: 85.6 us -> 0 us
  Pallas kernels: 0 us -> 74.3 us
  waiting for transfers between devices: 30 us -> 0 us
  other arithmetic: 26.2 us -> 0 us
  local copies, waits for them, and re-layouts: 32.8 us -> 9.87 us
  starting transfers between devices: 12.7 us -> 0 us
    psum x1 -> x0, blocking collectives: 296 us -> none  [per_device(): summed = lax.psum(slab[:, :, None, :] * selected[None, None, :, None], 'br')]
    dot_general x50 -> x0, matrix products: 85.6 us -> none  [the longest x10 24.2 us: head_grads(): jnp.dot(attention_low.T, kept_grad, preferred_element_type=jnp.float32)]
    pallas_call x0 -> x1, Pallas kernels: none -> 74.3 us  [fused(): pl.pallas_call(kernel, out_shape=(big, big, big, small, small), in_specs=...]
    all_to_all x3 -> x0, waiting for transfers between devices: 30 us -> none  [the longest x1 20.1 us: per_device(): lax.all_to_all(arranged, 'hd', split_axis=0, concat_axis=4, tiled=True)]
    reduce_sum x20 -> x0, other arithmetic: 16.2 us -> none  [the longest x10 12 us: head_grads(): jnp.sum(kept_grad.astype(jnp.float32) * output.astype(jnp.float32), axis=...]
    all_to_all x3 -> x0, starting transfers between devices: 12.7 us -> none  [the longest x1 4.84 us: per_device(): lax.all_to_all(own_slab(prefix_k), 'hd', split_axis=1, concat_axis=0, til...]
    unnamed x7 -> x15, local copies, waits for them, and re-layouts: 0.8 us -> 9.87 us
    reshape x6 -> x0, local copies, waits for them, and re-layouts: 8.99 us -> none  [the longest x1 4.54 us: per_device(): merged = spread.reshape(own_rows, 2, prompts, full_width)]
  transfers between devices with their start and end apart: 3 -> 0, of which waited for: 3 -> 0; matrix products, arithmetic and copies ran while one was open for 3% -> 0% of each run, Pallas kernels for 0% -> 0%
where the time goes in v2:
time: 85 us; the launch traced here: 84.8 us
  Pallas kernels  74.3 us (87%)
  local copies, waits for them, and re-layouts  9.87 us (12%)
    pallas_call x1, Pallas kernels, fused(): pl.pallas_call(kernel, out_shape=(big, big, big, small, small), in_specs=...  74.3 us
    unnamed x15, local copies, waits for them, and re-layouts  9.87 us

profile of v2, /device:TPU:1, one launch (start us, length us, event | category | flops | bytes accessed | tf_op | source)
XLA Modules:
  0.0 84.8 jit_solution(9898250993744179298)
XLA Ops:
  0.6 0.0 copy-start
  0.6 1.3 %copy-done = bf16[512,1280]{1,0:T(8,128)(2,1)S(1)} copy-done((bf16[512,1280]{1,0:T(8,128)(2,1)S(1)}, bf16[512,1280]{1,0:T(8,128)(2,1)}, u32[]{:S(2)}) %copy-start) | copy-done | bytes 1310744
  2.0 0.0 copy-start.1
  2.0 1.3 %copy-done.1 = bf16[512,1280]{1,0:T(8,128)(2,1)S(1)} copy-done((bf16[512,1280]{1,0:T(8,128)(2,1)S(1)}, bf16[512,1280]{1,0:T(8,128)(2,1)}, u32[]{:S(2)}) %copy-start.1) | copy-done | bytes 1310744
  3.3 0.0 copy-start.2
  3.3 0.7 copy-done.2
  3.9 0.0 copy-start.3
  3.9 0.7 copy-done.3
  4.6 0.0 copy-start.4
  4.6 0.7 copy-done.4
  5.2 74.3 %tree_grads.1 = (bf16[512,1280]{1,0:T(8,128)(2,1)S(1)}, bf16[512,1280]{1,0:T(8,128)(2,1)S(1)}, bf16[512,1280]{1,0:T(8,128)(2,1)S(1)}, bf16[2,64,5120]{2,1,0:T(8,128)(2,1)S(1)}, bf16[2,64,5120]{2,1,0:T(8,128)(2,1)S(1)}) custom-call(s32[1,4]{1,0:T(1,128)S(1)} %copy-done.2, s32[1,4]{1,0:T(1,128)S(1)} %copy-done.3, s32[64]{0:T(128)S(1)} %bitcast.1, ...), custom_call_target="tpu_custom_call" | custom-call | tf_op jit(solution)/shard_map/tree_grads/pallas_call | solution.py:372
  79.5 1.1 %copy.20 = bf16[512,1280]{1,0:T(8,128)(2,1)} copy(bf16[512,1280]{1,0:T(8,128)(2,1)S(1)} %get-tuple-element.10) | data formatting | bytes 2621440
  80.6 1.1 %copy.21 = bf16[512,1280]{1,0:T(8,128)(2,1)} copy(bf16[512,1280]{1,0:T(8,128)(2,1)S(1)} %get-tuple-element.11) | data formatting | bytes 2621440
  81.7 1.1 %copy.22 = bf16[512,1280]{1,0:T(8,128)(2,1)} copy(bf16[512,1280]{1,0:T(8,128)(2,1)S(1)} %get-tuple-element.12) | data formatting | bytes 2621440
  82.7 1.1 %copy.23 = bf16[2,64,5120]{2,1,0:T(8,128)(2,1)} copy(bf16[2,64,5120]{2,1,0:T(8,128)(2,1)S(1)} %get-tuple-element.13) | data formatting | bytes 2621440
  83.8 1.1 %copy.24 = bf16[2,64,5120]{2,1,0:T(8,128)(2,1)} copy(bf16[2,64,5120]{2,1,0:T(8,128)(2,1)S(1)} %get-tuple-element.14) | data formatting | bytes 2621440
Async XLA Ops:
  0.6 1.3 %copy-start = (bf16[512,1280]{1,0:T(8,128)(2,1)S(1)}, bf16[512,1280]{1,0:T(8,128)(2,1)}, u32[]{:S(2)}) copy-start(bf16[512,1280]{1,0:T(8,128)(2,1)} %q_hbm.1) | copy-start | bytes 3932164
  2.0 1.3 %copy-start.1 = (bf16[512,1280]{1,0:T(8,128)(2,1)S(1)}, bf16[512,1280]{1,0:T(8,128)(2,1)}, u32[]{:S(2)}) copy-start(bf16[512,1280]{1,0:T(8,128)(2,1)} %k_hbm.1) | copy-start | bytes 3932164
  3.3 0.7 copy-start.2
  3.9 0.7 copy-start.3
  4.6 0.7 copy-start.4

commit v3 on v2

v3 whole, which is shorter than its diff:
```python
import jax
import jax.numpy as jnp
from jax import lax
from jax.experimental import pallas as pl
from jax.experimental.pallas import tpu as pltpu
from jax.sharding import PartitionSpec as P

HS = 128
TILE = 128
BLOCKS = 4
PLEN = 256
PROMPTS = 2
ROWS = 512
HEADS = 10
COLS = 1280
GROUPS = 4
NY = 4
NZ = 8
BATCHES = HEADS // 2
OWN_ROWS = PLEN // GROUPS
SCALE = HS**-0.5
LOG2E = 1.4426950408889634
MESH = pl.DeviceIdType.MESH
VMEM = pltpu.VMEM
BF16 = jnp.bfloat16
F32 = jnp.float32
LAGS = (4, 14, 26, 36, 45, 62)
VMEM_BYTES = 47 << 20
AT_PARENTS = 64
AT_LENGTHS = 68
WORDS = 72


def place():
    br = lax.axis_index("br")
    return lax.axis_index("hd"), (br // 2) % NY, br // (2 * NY), br % 2


def device(x, y, z, core):
    return ((z * NY + y) * 2 + core, x)


def remote(src, dst, send, recv, who):
    return pltpu.make_async_remote_copy(
        src_ref=src, dst_ref=dst, send_sem=send, recv_sem=recv, device_id=who, device_id_type=MESH
    )


def dot(a, b):
    return jnp.dot(a, b, preferred_element_type=F32)


def dot_t(a, b):
    return lax.dot_general(a, b, (((1,), (1,)), ((), ())), preferred_element_type=F32)


def cols_of(h):
    return pl.ds(pl.multiple_of(h * HS, HS), HS)


def fill_bias(words, bias):
    key = lax.broadcasted_iota(jnp.int32, (TILE, TILE), 0)
    query = lax.broadcasted_iota(jnp.int32, (TILE, TILE), 1)
    reach = {}
    for b in range(BLOCKS):
        up = words[AT_PARENTS + b]
        for c in range(b):
            hit = (up == c).astype(jnp.int32)
            for mid in range(c + 1, b):
                hit = hit | ((up == mid).astype(jnp.int32) & reach[mid, c])
            reach[b, c] = hit
    for c in range(BLOCKS):
        for b in range(BLOCKS):
            if b > c:
                seen = key < reach[b, c] * words[AT_LENGTHS + c]
            elif b == c:
                seen = (key < words[AT_LENGTHS + c]) & (key <= query)
            else:
                seen = key < 0
            bias[c * TILE : (c + 1) * TILE, b * TILE : (b + 1) * TILE] = jnp.where(seen, 0.0, -1e30)


def kernel(
    words_hbm, q_hbm, k_hbm, v_hbm, o_hbm, g_hbm, pk_hbm, pv_hbm,
    dq, dk, dv, sums_k, sums_v,
    words, q, k, v, o, g, t0, t1, t2, t3, t4, t5, t6, t7, held, pre, bias, e_tree, g_tree, att_pre, ds_pre, stats,
    part, got1, line, got2,
    word_sem, table_sem, load_sem, pre_send, pre_recv, s1_send, s1_recv, s2_send, s2_recv,
    s4_send, s4_recv, s5_send, s5_recv, s6_send, s6_recv,
):
    x, y, z, core = place()
    mate = device(x, y, z, 1 - core)
    br = lax.axis_index("br")

    barrier = pltpu.get_barrier_semaphore()
    partners = [device(x, y, (z + d) % NZ, core) for d in (4, 3, 5, 2, 6)]
    partners += [
        device((x + dx) % GROUPS, (y + dy) % NY, z, c)
        for dx in (2, 1, 3, 0)
        for dy in (2, 1, 3, 0)
        for c in ((core, 1 - core) if dx or dy else (1 - core,))
    ]
    partners += [device(x, y, (z + d) % NZ, core) for d in (1, 7)]
    for who in partners:
        pl.semaphore_signal(barrier, inc=1, device_id=who, device_id_type=MESH)

    get_words = pltpu.make_async_copy(words_hbm, words, word_sem)
    get_words.start()
    table = ((t0, t1, t2, t3), (t4, t5, t6, t7))
    order = [(x + d) % GROUPS for d in (2, 1, 3, 0)]
    tables = []
    for a, src in enumerate((pk_hbm, pv_hbm)):
        for i, to in enumerate(order):
            at = pl.ds(pl.multiple_of(to * COLS, COLS), COLS)
            tables.append(pltpu.make_async_copy(src.at[:, :, at], table[a][i], table_sem.at[a, i]))
            tables[-1].start()
    get_words.wait()
    mine = words[br]

    def gather(a, i):
        d = (2, 1, 3)[i]
        return remote(
            held.at[a, i], pre.at[a, own_rows], pre_send.at[a, i], pre_recv.at[a, i],
            device((x + d) % GROUPS, y, z, core),
        )

    own_rows = pl.ds(pl.multiple_of(x * OWN_ROWS, OWN_ROWS), OWN_ROWS)
    pl.semaphore_wait(barrier, len(partners))
    loads = []
    for a in range(2):
        for i in range(GROUPS):
            tables[GROUPS * a + i].wait()
            if i < 3:
                held[a, i] = table[a][i][mine]
                gather(a, i).start()
            else:
                pre[a, own_rows] = table[a][i][mine]
        if a == 0:
            for i, (src, dst) in enumerate(((q_hbm, q), (k_hbm, k), (g_hbm, g), (o_hbm, o), (v_hbm, v))):
                loads.append(pltpu.make_async_copy(src, dst, load_sem.at[i]))
                loads[-1].start()
    fill_bias(words, bias)
    for load in loads:
        load.wait()

    row = lax.broadcasted_iota(jnp.int32, (TILE, HS), 0)

    @pl.loop(0, HEADS)
    def _(h):
        cols = cols_of(h)
        for pair in range(2):
            rows = pl.ds(256 * pair, 256)
            known = 256 * (pair + 1)
            base = 256 * pair
            qp = q[rows, cols]
            for b in (2 * pair, 2 * pair + 1):
                at = pl.ds(b * TILE, TILE)
                g[at, cols] = jnp.where(row < words[AT_LENGTHS + b], g[at, cols], jnp.zeros((), BF16))
            gp = g[rows, cols]
            row_dot = jnp.sum((gp.astype(F32) * o[rows, cols].astype(F32)).T, axis=0, keepdims=True)
            s = dot_t(k[:known, cols], qp) * (SCALE * LOG2E) + bias[:known, rows]
            top = jnp.max(s, axis=0, keepdims=True)
            e = jnp.exp2(s - top)
            stats[h, pair, 0:1] = top
            stats[h, pair, 1:2] = jnp.sum(e, axis=0, keepdims=True)
            stats[h, pair, 2:3] = row_dot
            e_tree[h, base : base + known] = e
            g_tree[h, base : base + known] = e * (dot_t(v[:known, cols], gp) - row_dot)

    for i in range(3):
        gather(0, i).wait()

    def value_part(h):
        cols = cols_of(h)
        value_sum = None
        for pair in range(2):
            rows = pl.ds(256 * pair, 256)
            top_tree, sum_tree = stats[h, pair, 0:1], stats[h, pair, 1:2]
            s = dot_t(pre[0, :, cols], q[rows, cols]) * (SCALE * LOG2E)
            top = jnp.maximum(jnp.max(s, axis=0, keepdims=True), top_tree)
            e = jnp.exp2(s - top)
            carry = jnp.exp2(top_tree - top)
            share = 1.0 / (jnp.sum(e, axis=0, keepdims=True) + sum_tree * carry)
            stats[h, pair, 3:4] = carry * share
            att = e * share
            att_pre[h, pair] = att
            got = dot(att.astype(BF16), g[rows, cols])
            value_sum = got if pair == 0 else value_sum + got
        part[h // 4, h % 4] = value_sum.astype(BF16)

    def key_part(i):
        h, u = (i + 8) % HEADS, i + HEADS
        cols = cols_of(h)
        key_sum = None
        for pair in range(2):
            rows = pl.ds(256 * pair, 256)
            row_dot = stats[h, pair, 2:3]
            ds = (att_pre[h, pair] * (dot_t(pre[1, :, cols], g[rows, cols]) - row_dot)).astype(BF16)
            ds_pre[h, pair] = ds
            got = dot(ds, q[rows, cols])
            key_sum = got if pair == 0 else key_sum + got
        part[u // 4, u % 4] = (key_sum * SCALE).astype(BF16)

    def tree_part(h):
        cols = cols_of(h)
        keys, pre_keys = k[:, cols].T, pre[0, :, cols].T
        first_k = first_v = None
        for pair in range(2):
            rows = pl.ds(256 * pair, 256)
            known = 256 * (pair + 1)
            base = 256 * pair
            qp, gp = q[rows, cols], g[rows, cols]
            factor = stats[h, pair, 3:4]
            att = (e_tree[h, base : base + known] * factor).astype(BF16)
            ds = (g_tree[h, base : base + known] * factor).astype(BF16)
            got_k, got_v = dot(ds, qp), dot(att, gp)
            dq_t = dot(pre_keys, ds_pre[h, pair]) + dot(keys[:, :known], ds)
            dq[rows, cols] = (dq_t.T * SCALE).astype(BF16)
            if pair == 0:
                first_k, first_v = got_k, got_v
            else:
                dk[:256, cols] = ((first_k + got_k[:256]) * SCALE).astype(BF16)
                dv[:256, cols] = (first_v + got_v[:256]).astype(BF16)
                dk[256:, cols] = (got_k[256:] * SCALE).astype(BF16)
                dv[256:, cols] = got_v[256:].astype(BF16)

    def slot_of(dx, dy, off):
        return (dx * NY + dy) * 2 + off

    def sent(ref, sem):
        remote(ref, ref, sem, s1_recv.at[0], mate).wait_send()

    def landed(ref, sem):
        remote(ref, ref, s1_send.at[0], sem, mate).wait_recv()

    def with_unit(j, yy, work):
        u = NY * j + yy
        late = u // HEADS
        cols = cols_of((u - 2 * late) % HEADS)
        for which, ref in enumerate((sums_v, sums_k)):

            @pl.when(late == which)
            def _(ref=ref):
                work(ref, cols)

    def rows_of(zz):
        return zz // 4, pl.ds(pl.multiple_of(zz % 4 * 16, 16), 16)

    def far1(j, dx, dy):
        to_x, to_y = (x + dx) % GROUPS, (y + dy) % NY
        own = j % 2
        rows = pl.ds(pl.multiple_of(to_x * OWN_ROWS, OWN_ROWS), OWN_ROWS)
        return remote(
            part.at[j, to_y, rows], got1.at[j, slot_of(dx, dy, (core + own) % 2)], s1_send.at[j], s1_recv.at[j],
            device(to_x, to_y, z, own),
        )

    def far2(j, d):
        to = (z + d) % NZ
        return remote(line.at[j, to], got2.at[j, d - 1], s2_send.at[j], s2_recv.at[j], device(x, y, to, core))

    def far4(j, d, ref):
        return remote(ref, ref, s4_send.at[j], s4_recv.at[j], device(x, y, (z + d) % NZ, core))

    def far5(j, d, ref):
        return remote(ref, ref, s5_send.at[j], s5_recv.at[j, d - 1], device(x, (y + d) % NY, z, core))

    def far6(j, ref):
        return remote(ref, ref, s6_send.at[j], s6_recv.at[j], mate)

    def send1(j):
        for dy in (2, 1, 3, 0):
            for dx in (2, 1, 3, 0):
                if dx or dy:
                    far1(j, dx, dy).start()

        @pl.when(core == j % 2)
        def _():
            got1[j, 0] = part[j, y, own_rows]

        @pl.when(core != j % 2)
        def _():
            far1(j, 0, 0).start()

    def sum1(j):
        landed(got1.at[j, pl.ds(1, 2 * NY * GROUPS - 1)], s1_recv.at[j])
        weights = []
        for dy in range(NY):
            for off in range(2):
                whose = words[(z * NY + (y + NY - dy) % NY) * 2 + (core + off) % 2]
                weights.append([(whose == p).astype(F32) for p in range(PROMPTS)])

        @pl.loop(0, 16)
        def _(tile):
            dx, rt = tile // 4, tile % 4
            rows = pl.ds(pl.multiple_of(rt * 16, 16), 16)
            sums = [None] * PROMPTS
            for i in range(2 * NY):
                term = got1[j, dx * 2 * NY + i, rows].astype(F32)
                for p in range(PROMPTS):
                    scaled = weights[i][p] * term
                    sums[p] = scaled if i == 0 else sums[p] + scaled
            for p in range(PROMPTS):
                line[j, 4 * p + rt, (x + GROUPS - dx) % GROUPS] = sums[p].astype(BF16)

        for d in (4, 3, 5, 2, 6, 1, 7):
            far2(j, d).start()

    def sum2(j):
        landed(got2.at[j], s2_recv.at[j])
        sent(got2.at[j], s2_send.at[j])
        p, rows = rows_of(z)

        def work(sums, cols):
            for xx in range(GROUPS):
                total = line[j, z, xx].astype(F32)
                for d in range(1, NZ):
                    total += got2[j, d - 1, xx].astype(F32)
                sums[xx, p, rows, cols] = total.astype(BF16)
            for d in (4, 3, 5, 2, 6, 1, 7):
                far4(j, d, sums.at[:, p, rows, cols]).start()

        with_unit(j, y, work)

    def share4(j):
        landed(got2.at[j], s4_recv.at[j])

        def work(sums, cols):
            ref = sums.at[:, :, :, cols]
            for d in (2, 1, 3):
                far5(j, d, ref).start()
            far6(j, ref).start()

        with_unit(j, y, work)

    def share5(j):
        for d in (1, 3, 2):
            landed(got1.at[j, pl.ds(0, 2 * NY)], s5_recv.at[j, d - 1])
            with_unit(j, (y + NY - d) % NY, lambda sums, cols: far6(j, sums.at[:, :, :, cols]).start())

    def finish(j):
        @pl.when(core != j % 2)
        def _():
            landed(got1.at[j], s6_recv.at[j])

    def stage(step, lag, whole, work):
        j = (step - lag) // 4
        due = (step >= lag) & (step < lag + 4 * BATCHES) & ((step - lag) % 4 == 0)
        if not whole:
            due = due & (core == j % 2)

        @pl.when(due)
        def _():
            work(j)

    @pl.loop(0, 4 * BATCHES + LAGS[-1])
    def _(step):
        @pl.when(step < HEADS)
        def _():
            value_part(step)

        @pl.when(step == HEADS)
        def _():
            for i in range(3):
                gather(1, i).wait()

        @pl.when((step >= HEADS) & (step < 2 * HEADS))
        def _():
            key_part(step - HEADS)

        stage(step + 1, LAGS[0], True, send1)

        @pl.when((step >= 2 * HEADS) & (step < 3 * HEADS))
        def _():
            tree_part(step - 2 * HEADS)

        stage(step, LAGS[1], False, sum1)
        stage(step, LAGS[2], False, sum2)
        stage(step, LAGS[3], False, share4)
        stage(step, LAGS[4], False, share5)
        stage(step, LAGS[5], True, finish)

    @pl.loop(0, BATCHES)
    def _(j):
        sent(got1.at[j, pl.ds(0, NY * GROUPS - 1)], s1_send.at[j])

        @pl.when(core != j % 2)
        def _():
            sent(got1.at[j, 0], s1_send.at[j])

        @pl.when(core == j % 2)
        def _():
            sent(got2.at[j], s4_send.at[j])
            sent(got1.at[j, pl.ds(0, 3 * 2 * NY)], s5_send.at[j])
            sent(got1.at[j], s6_send.at[j])


def fused(words, q, k, v, o, g, prefix_k, prefix_v):
    smem = pltpu.SMEM
    hbm = pl.BlockSpec(memory_space=pltpu.HBM)
    vmem = pl.BlockSpec(memory_space=VMEM)
    big = jax.ShapeDtypeStruct((ROWS, COLS), BF16)
    small = jax.ShapeDtypeStruct((GROUPS, PROMPTS, OWN_ROWS, COLS), BF16)
    sem = pltpu.SemaphoreType.DMA

    def pair(*shape):
        return [sem(shape), sem(shape)]

    return pl.pallas_call(
        kernel,
        out_shape=(big, big, big, small, small),
        in_specs=[hbm] * 8,
        out_specs=(vmem,) * 5,
        scratch_shapes=[smem((WORDS,), jnp.int32)]
        + [VMEM((ROWS, COLS), BF16)] * 5
        + [VMEM((PROMPTS, OWN_ROWS, COLS), BF16)] * (2 * GROUPS)
        + [
            VMEM((2, GROUPS - 1, OWN_ROWS, COLS), BF16),
            VMEM((2, PLEN, COLS), BF16),
            VMEM((ROWS, ROWS), F32),
            VMEM((HEADS, 768, 256), F32),
            VMEM((HEADS, 768, 256), F32),
            VMEM((HEADS, 2, PLEN, 256), F32),
            VMEM((HEADS, 2, PLEN, 256), BF16),
            VMEM((HEADS, 2, 8, 256), F32),
            VMEM((BATCHES, NY, PLEN, HS), BF16),
            VMEM((BATCHES, 2 * NY * GROUPS, OWN_ROWS, HS), BF16),
            VMEM((BATCHES, NZ, GROUPS, 16, HS), BF16),
            VMEM((BATCHES, NZ - 1, GROUPS, 16, HS), BF16),
            sem,
            sem((2, GROUPS)),
            sem((5,)),
        ]
        + pair(2, GROUPS - 1)
        + pair(BATCHES)
        + pair(BATCHES)
        + pair(BATCHES)
        + [sem((BATCHES,)), sem((BATCHES, NY - 1))]
        + pair(BATCHES),
        compiler_params=pltpu.CompilerParams(
            collective_id=1, has_side_effects=True, vmem_limit_bytes=VMEM_BYTES
        ),
        name="tree_grads",
    )(words, q, k, v, o, g, prefix_k, prefix_v)


def write_kernel(dq, dk, dv, sums_k, sums_v, dq_out, dk_out, dv_out, key_out, value_out, sems):
    pairs = [(dq, dq_out), (dk, dk_out), (dv, dv_out)]
    for sums, out in ((sums_k, key_out), (sums_v, value_out)):
        pairs += [(sums.at[xx], out.at[:, :, pl.ds(xx * COLS, COLS)]) for xx in range(GROUPS)]
    copies = [pltpu.make_async_copy(src, dst, sems.at[i]) for i, (src, dst) in enumerate(pairs)]
    for copy in copies:
        copy.start()
    for copy in copies:
        copy.wait()


def write(dq, dk, dv, sums_k, sums_v):
    big = jax.ShapeDtypeStruct((ROWS, COLS), BF16)
    small = jax.ShapeDtypeStruct((PROMPTS, OWN_ROWS, GROUPS * COLS), BF16)
    return pl.pallas_call(
        write_kernel,
        out_shape=(big, big, big, small, small),
        in_specs=[pl.BlockSpec(memory_space=VMEM)] * 5,
        out_specs=(pl.BlockSpec(memory_space=pltpu.HBM),) * 5,
        scratch_shapes=[pltpu.SemaphoreType.DMA((3 + 2 * GROUPS,))],
        compiler_params=pltpu.CompilerParams(vmem_limit_bytes=1 << 20),
        name="write",
    )(dq, dk, dv, sums_k, sums_v)


def per_device(q, k, v, o, g, prefix_k, prefix_v, parents, lengths, prompt_of):
    words = jnp.concatenate([prompt_of[:, 0], parents[0], lengths[0]])
    return write(*fused(words, q, k, v, o, g, prefix_k, prefix_v))


def solution(mesh):
    split = P("br", "hd")
    held = P(None, "hd", None)
    return jax.shard_map(
        per_device,
        mesh=mesh,
        in_specs=(split,) * 5 + (held, held, P("br", None), P("br", None), P()),
        out_specs=(split,) * 3 + (held, held),
        check_vma=False,
    )
```

time: 85 us -> 69.2 us (0.81)
  local copies, waits for them, and re-layouts: 9.87 us -> 0 us
  Pallas kernels: 74.3 us -> 67.7 us
    unnamed x15 -> x0, local copies, waits for them, and re-layouts: 9.87 us -> none
    pallas_call x1, Pallas kernels: 74.3 us -> 64.9 us  [fused(): pl.pallas_call(kernel, out_shape=(big, big, big, small, small), in_specs=...]
    pallas_call x0 -> x1, Pallas kernels: none -> 2.82 us  [write(): pl.pallas_call(write_kernel, out_shape=(big, big, big, small, small), in_...]
where the time goes in v3:
time: 69.2 us; the launch traced here: 69.1 us
  Pallas kernels  67.7 us (98%)
  other arithmetic  0.76 us (1%)
    pallas_call x1, Pallas kernels, fused(): pl.pallas_call(kernel, out_shape=(big, big, big, small, small), in_specs=...  64.9 us
    pallas_call x1, Pallas kernels, write(): pl.pallas_call(write_kernel, out_shape=(big, big, big, small, small), in_...  2.82 us

profile of v3, /device:TPU:1, one launch (start us, length us, event | category | flops | bytes accessed | tf_op | source)
XLA Modules:
  0.0 69.1 jit_solution(16583718009146039740)
XLA Ops:
  0.6 0.8 %pad_add_fusion.words_hbm = s32[72]{0:T(128)S(1)} fusion(s32[4]{0:T(128)} %bitcast.3, s32[4]{0:T(128)} %bitcast.4, s32[64]{0:T(128)} %bitcast.5), kind=kLoop, calls=%fused_computation | loop fusion | flops 144 | bytes 576 | tf_op jit(solution)/shard_map/concatenate | solution.py:473
  1.4 64.9 %tree_grads.1 = (bf16[512,1280]{1,0:T(8,128)(2,1)S(1)}, bf16[512,1280]{1,0:T(8,128)(2,1)S(1)}, bf16[512,1280]{1,0:T(8,128)(2,1)S(1)}, bf16[4,2,64,1280]{3,2,1,0:T(8,128)(2,1)S(1)}, bf16[4,2,64,1280]{3,2,1,0:T(8,128)(2,1)S(1)}) custom-call(s32[72]{0:T(128)S(1)} %pad_add_fusion.words_hbm, bf16[512,1280]{1,0:T(8,128)(2,1)} %q_hbm.1, bf16[512,1280]{1,0:T(8,128)(2,1)} %k_hbm.1, ...), custom_call_target="tpu_custom_call" | custom-call | tf_op jit(solution)/shard_map/tree_grads/pallas_call | solution.py:409
  66.3 2.8 %write.1 = (bf16[512,1280]{1,0:T(8,128)(2,1)}, bf16[512,1280]{1,0:T(8,128)(2,1)}, bf16[512,1280]{1,0:T(8,128)(2,1)}, bf16[2,64,5120]{2,1,0:T(8,128)(2,1)}, bf16[2,64,5120]{2,1,0:T(8,128)(2,1)}) custom-call(bf16[512,1280]{1,0:T(8,128)(2,1)S(1)} %get-tuple-element.10.dq, bf16[512,1280]{1,0:T(8,128)(2,1)S(1)} %get-tuple-element.11.dk, ...), custom_call_target="tpu_custom_call" | custom-call | tf_op jit(solution)/shard_map/write/pallas_call | solution.py:461

commit v4 on v3

--- a/solution.py
+++ b/solution.py
@@ -24,7 +24,7 @@
 VMEM = pltpu.VMEM
 BF16 = jnp.bfloat16
 F32 = jnp.float32
-LAGS = (4, 14, 26, 36, 45, 62)
+LAGS = (4, 11, 20, 28, 36, 52)
 VMEM_BYTES = 47 << 20
 AT_PARENTS = 64
 AT_LENGTHS = 68

time: 69.2 us -> 67.8 us (0.980)
  Pallas kernels: 67.7 us -> 66.3 us
    pallas_call x1, Pallas kernels: 64.9 us -> 63.4 us  [fused(): pl.pallas_call(kernel, out_shape=(big, big, big, small, small), in_specs=...]
where the time goes in v4:
time: 67.8 us; the launch traced here: 67.7 us
  Pallas kernels  66.3 us (98%)
  other arithmetic  0.76 us (1%)
    pallas_call x1, Pallas kernels, fused(): pl.pallas_call(kernel, out_shape=(big, big, big, small, small), in_specs=...  63.4 us
    pallas_call x1, Pallas kernels, write(): pl.pallas_call(write_kernel, out_shape=(big, big, big, small, small), in_...  2.82 us

profile of v4, /device:TPU:1, one launch (start us, length us, event | category | flops | bytes accessed | tf_op | source)
XLA Modules:
  0.0 67.7 jit_solution(17851406740789379680)
XLA Ops:
  0.6 0.8 %pad_add_fusion.words_hbm = s32[72]{0:T(128)S(1)} fusion(s32[4]{0:T(128)} %bitcast.3, s32[4]{0:T(128)} %bitcast.4, s32[64]{0:T(128)} %bitcast.5), kind=kLoop, calls=%fused_computation | loop fusion | flops 144 | bytes 576 | tf_op jit(solution)/shard_map/concatenate | solution.py:473
  1.4 63.4 %tree_grads.1 = (bf16[512,1280]{1,0:T(8,128)(2,1)S(1)}, bf16[512,1280]{1,0:T(8,128)(2,1)S(1)}, bf16[512,1280]{1,0:T(8,128)(2,1)S(1)}, bf16[4,2,64,1280]{3,2,1,0:T(8,128)(2,1)S(1)}, bf16[4,2,64,1280]{3,2,1,0:T(8,128)(2,1)S(1)}) custom-call(s32[72]{0:T(128)S(1)} %pad_add_fusion.words_hbm, bf16[512,1280]{1,0:T(8,128)(2,1)} %q_hbm.1, bf16[512,1280]{1,0:T(8,128)(2,1)} %k_hbm.1, ...), custom_call_target="tpu_custom_call" | custom-call | tf_op jit(solution)/shard_map/tree_grads/pallas_call | solution.py:409
  64.8 2.8 %write.1 = (bf16[512,1280]{1,0:T(8,128)(2,1)}, bf16[512,1280]{1,0:T(8,128)(2,1)}, bf16[512,1280]{1,0:T(8,128)(2,1)}, bf16[2,64,5120]{2,1,0:T(8,128)(2,1)}, bf16[2,64,5120]{2,1,0:T(8,128)(2,1)}) custom-call(bf16[512,1280]{1,0:T(8,128)(2,1)S(1)} %get-tuple-element.10.dq, bf16[512,1280]{1,0:T(8,128)(2,1)S(1)} %get-tuple-element.11.dk, ...), custom_call_target="tpu_custom_call" | custom-call | tf_op jit(solution)/shard_map/write/pallas_call | solution.py:461
